TPU v7x, 256 devices: a whole 4x4x8 slice. The times are simulated.
256 devices in a mesh: seq: 64 (over y, z, core), kvh: 4 (over x).
Axes of the slice: x: 4, y: 4, z: 8, core: 2. Of those that a mesh axis runs over, the one named last changes fastest.
Arguments:
- queries: bfloat16 [128, 64, 128], P('seq', 'kvh')
- cache_keys: bfloat16 [131072, 8, 128], P('seq', 'kvh'), may hold values from -6 to 6
- cache_values: bfloat16 [131072, 8, 128], P('seq', 'kvh'), may hold values from -6 to 6
- new_keys: bfloat16 [128, 8, 128], P('seq', 'kvh'), may hold values from -6 to 6
- new_values: bfloat16 [128, 8, 128], P('seq', 'kvh'), may hold values from -6 to 6
- doc_start: int32 [128, 2], replicated, may hold values from 0 to 255, as said below
- doc_count: int32 [128, 2], replicated, may hold values from 1 to 64
Outputs:
- attended: bfloat16 [128, 64, 128], P('seq', 'kvh')
Inputs may be any that keep to these rules, and one draw needn't show every extreme that they name: doc_start[r, i] + doc_count[r, i] <= 256.
All inputs are finite; a program needn't handle non-finite values.
Results may differ from a plain program's by a relative error of at most 0.0048.
Values may be sent and summed in bfloat16 or wider, within the bound.
A program may use at most 256 MiB of HBM per device.

v0:
```python
import jax
import jax.numpy as jnp
from jax import lax
from jax.sharding import PartitionSpec as P

QH = 64
KVH = 8
HD = 128
BLOCK = 512


NEG = -1e30


def combined_all(value, axis, join):
    pieces = jax.tree.map(lambda part: lax.all_gather(part, axis), value)
    head = jax.tree.map(lambda part: part[0], pieces)
    tail = jax.tree.map(lambda part: part[1:], pieces)
    so_far, _ = lax.scan(lambda so_far, slab: (join(so_far, slab), None), head, tail)
    return so_far


def combine_pair(first, second):
    out_a, top_a, total_a = first
    out_b, top_b, total_b = second
    high = jnp.maximum(top_a, top_b)
    weight_a = jnp.exp(top_a - high)
    weight_b = jnp.exp(top_b - high)
    return (
        out_a * weight_a[..., None] + out_b * weight_b[..., None],
        high,
        total_a * weight_a + total_b * weight_b,
    )


def per_device(queries, cache_keys, cache_values, new_keys, new_values, doc_start, doc_count):
    group = QH // KVH
    scale = HD ** (-0.5)
    rows_local = queries.shape[0]
    heads_local = queries.shape[1]
    kv_local = cache_keys.shape[1]
    tokens_local = cache_keys.shape[0]
    blocks_local = tokens_local // BLOCK
    every_query = lax.all_gather(queries, "seq", axis=0, tiled=True)
    rows_all = every_query.shape[0]
    q_four = every_query.reshape(rows_all, kv_local, group, HD)
    segment = lax.axis_index("seq")
    blocks = segment * blocks_local + jnp.arange(blocks_local, dtype=jnp.int32)
    inside = (doc_start[:, :, None] <= blocks[None, None, :]) & (
        blocks[None, None, :] < (doc_start + doc_count)[:, :, None]
    )
    mask = jnp.repeat(jnp.any(inside, axis=1), BLOCK, axis=1)[None, None]
    scores = (
        jnp.einsum("rgjd,tgd->gjrt", q_four, cache_keys, preferred_element_type=jnp.float32) * scale
    )
    top = jnp.max(jnp.where(mask, scores, NEG), axis=-1)
    probs = jnp.where(mask, jnp.exp(scores - top[..., None]), 0.0)
    total = jnp.sum(probs, axis=-1)
    out = jnp.einsum(
        "gjrt,tgd->rgjd",
        probs.astype(jnp.bfloat16),
        cache_values,
        preferred_element_type=jnp.float32,
    )
    out = out.reshape(rows_all, heads_local, HD)
    top = jnp.transpose(top, (2, 0, 1)).reshape(rows_all, heads_local)
    total = jnp.transpose(total, (2, 0, 1)).reshape(rows_all, heads_local)
    whole, high, norm = combined_all((out, top, total), "seq", combine_pair)
    first_row = segment * rows_local
    whole = lax.dynamic_slice_in_dim(whole, first_row, rows_local, 0)
    high = lax.dynamic_slice_in_dim(high, first_row, rows_local, 0)
    norm = lax.dynamic_slice_in_dim(norm, first_row, rows_local, 0)
    q_own = queries.reshape(rows_local, kv_local, group, HD)
    own = (
        jnp.einsum("rgjd,rgd->rgj", q_own, new_keys, preferred_element_type=jnp.float32).reshape(
            rows_local, heads_local
        )
        * scale
    )
    high_two = jnp.maximum(high, own)
    keep = jnp.exp(high - high_two)
    fresh = jnp.exp(own - high_two)
    value_new = jnp.broadcast_to(
        new_values.astype(jnp.float32)[:, :, None, :], (rows_local, kv_local, group, HD)
    ).reshape(rows_local, heads_local, HD)
    whole = whole * keep[..., None] + fresh[..., None] * value_new
    norm = norm * keep + fresh
    return (whole / norm[..., None]).astype(jnp.bfloat16)


def solution(mesh):
    placed = (
        P("seq", "kvh", None),
        P("seq", "kvh", None),
        P("seq", "kvh", None),
        P("seq", "kvh", None),
        P("seq", "kvh", None),
        P(),
        P(),
    )
    return jax.shard_map(
        per_device, mesh=mesh, in_specs=placed, out_specs=P("seq", "kvh", None), check_vma=False
    )
```

profile of v0, /device:TPU:1, one launch (start us, length us, event | category | flops | bytes accessed | tf_op | source)
XLA Modules:
  0.0 509.5 jit_solution(2127204806637251632)
XLA Ops:
  6.5 55.0 %all_gather.12 = bf16[128,16,128]{2,1,0:T(8,128)(2,1)S(1)} all-gather(bf16[2,16,128]{2,1,0:T(8,128)(2,1)} %param.9), channel_id=1, replica_groups=mesh['seq'=64,'kvh'=4] {'seq'}, dimensions={0}, use_global_device_ids=true | all-gather | bytes 532480 | tf_op jit(solution)/shard_map/all_gather | solution.py:44
  63.2 8.4 %fusion.3 = (f32[2,8,128]{2,1,0:T(8,128)S(1)}, f32[2,2048,128,8]{2,1,3,0:T(8,128)}) fusion(pred[128,2048]{0,1:T(8,128)(4,1)S(1)} %bitcast.68, bf16[128,2,8,128]{3,0,2,1:T(8,128)(2,1)S(1)} %bitcast.71, bf16[2048,2,128,1]{2,1,0,3:T(2,128)(2,1)} %bitcast.73), kind=kOutput, calls=%fused_computation.12 | convolution fusion | flops 1086322688 | bytes 18620416 | tf_op jit(solution)/shard_map/rgjd,tgd->gjrt/dot_general | solution.py:54
  71.7 8.5 %fusion.8 = f32[2,8,128,128]{3,2,1,0:T(8,128)S(1)} fusion(f32[2,2048,128,8]{2,1,3,0:T(8,128)} %get-tuple-element.92, f32[2,8,128]{2,1,0:T(8,128)S(1)} %get-tuple-element.91, pred[128,2048]{0,1:T(8,128)(4,1)S(1)} %bitcast.69, bf16[2048,2,128,1]{2,1,0,3:T(2,128)(2,1)S(1)} %bitcast.67), kind=kOutput, calls=%fused_computation.17 | convolution fusion | flops 1090519040 | bytes 19144704 | tf_op jit(solution)/shard_map/gjrt,tgd->rgjd/dot_general | solution.py:59
  82.1 9.1 %fusion.6 = f32[2,8,128]{2,1,0:T(8,128)S(1)} fusion(f32[2,2048,128,8]{2,1,3,0:T(8,128)} %get-tuple-element.92, f32[2,8,128]{2,1,0:T(8,128)S(1)} %get-tuple-element.91, pred[128,2048]{0,1:T(8,128)(4,1)S(1)} %bitcast.70), kind=kLoop, calls=%fused_computation.15 | loop fusion | flops 16775168 | bytes 17055744 | tf_op jit(solution)/shard_map/reduce_sum | solution.py:58
  91.2 49.4 %all_gather.15 = f32[64,128,16]{1,2,0:T(8,128)S(1)} all-gather(f32[1,128,16]{1,2,0:T(8,128)S(1)} %bitcast.75), channel_id=1, replica_groups=mesh['seq'=64,'kvh'=4] {'seq'}, dimensions={0}, use_global_device_ids=true | all-gather | bytes 532480 | tf_op jit(solution)/shard_map/all_gather | solution.py:16
  140.7 48.1 %all_gather.14 = f32[64,128,16]{1,2,0:T(8,128)S(1)} all-gather(f32[1,128,16]{1,2,0:T(8,128)S(1)} %bitcast.74), channel_id=1, replica_groups=mesh['seq'=64,'kvh'=4] {'seq'}, dimensions={0}, use_global_device_ids=true | all-gather | bytes 532480 | tf_op jit(solution)/shard_map/all_gather | solution.py:16
  189.0 129.4 %all-gather.2.cloned.1.call-done = f32[64,128,16,128]{3,2,1,0:T(8,128)} async-done(((f32[1,128,16,128]{3,2,1,0:T(8,128)}), f32[64,128,16,128]{3,2,1,0:T(8,128)}) %all-gather.2.cloned.1.call-update) | async-done | bytes 67108880 | tf_op jit(solution)/shard_map/all_gather | solution.py:16
  319.7 43.8 %slice.28 = f32[63,128,16,128]{3,2,1,0:T(8,128)} slice(f32[64,128,16,128]{3,2,1,0:T(8,128)} %all-gather.2.cloned.1.call-done), slice={[1:64], [0:128], [0:16], [0:128]} | slice | bytes 132120576 | tf_op jit(solution)/shard_map/slice | solution.py:18
  363.4 138.5 %while.14 = (s32[]{:T(128)}, f32[128,16,128]{2,1,0:T(8,128)S(1)}, f32[128,16]{1,0:T(8,128)S(1)}, f32[128,16]{1,0:T(8,128)S(1)}, f32[63,128,16]{1,2,0:T(8,128)S(1...) while((s32[]{:T(128)}, f32[128,16,128]{2,1,0:T(8,128)S(1)}, ...), condition=%wide.region_4.5_spmd, body=%wide.region_3.4_spmd.sunk | while | flops 798722 | bytes 3293285 | solution.py:19
  368.1 1.9 fusion.31
  370.3 1.9 fusion.31
  372.5 1.9 fusion.31
  374.7 1.9 fusion.31
  376.9 1.9 fusion.31
  379.1 1.9 fusion.31
  381.3 1.9 fusion.31
  383.5 1.9 fusion.31
  385.7 1.9 fusion.31
  387.9 1.9 fusion.31
  390.1 1.9 fusion.31
  392.3 1.9 fusion.31
  394.5 1.9 fusion.31
  396.7 1.9 fusion.31
  398.9 1.9 fusion.31
  401.1 1.9 fusion.31
  403.3 1.9 fusion.31
  409.9 1.9 fusion.31
  412.1 1.9 fusion.31
  414.3 1.9 fusion.31
  416.5 1.9 fusion.31
  418.7 1.9 fusion.31
  420.9 1.9 fusion.31
  (323 shorter events, 98.7 us)
Async XLA Ops:
  6.5 65.1 %copy-start = (bf16[2048,2,128]{2,1,0:T(2,128)(2,1)S(1)}, bf16[2048,2,128]{2,1,0:T(2,128)(2,1)}, u32[]{:S(2)}) copy-start(bf16[2048,2,128]{2,1,0:T(2,128)(2,1)} %param.11) | copy-start | bytes 3145732
  6.5 311.8 %all-gather.2.cloned.1.call-start = ((), (), s32[]{:S(2)}) async-start(), calls=%async_computation | async-start | bytes 68157440 | tf_op jit(solution)/shard_map/all_gather | solution.py:16
  71.7 10.1 %copy-start.2 = (bf16[2,16,128]{2,1,0:T(8,128)(2,1)S(1)}, bf16[2,16,128]{2,1,0:T(8,128)(2,1)}, u32[]{:S(2)}) copy-start(bf16[2,16,128]{2,1,0:T(8,128)(2,1)} %param.9) | copy-start | bytes 24580
  71.7 10.2 %copy-start.4 = (bf16[2,2,128]{2,1,0:T(2,128)(2,1)S(1)}, bf16[2,2,128]{2,1,0:T(2,128)(2,1)}, u32[]{:S(2)}) copy-start(bf16[2,2,128]{2,1,0:T(2,128)(2,1)} %param.12) | copy-start | bytes 3076
  71.7 10.4 %copy-start.3 = (bf16[2,2,128]{2,1,0:T(2,128)(2,1)S(1)}, bf16[2,2,128]{2,1,0:T(2,128)(2,1)}, u32[]{:S(2)}) copy-start(bf16[2,2,128]{2,1,0:T(2,128)(2,1)} %param.13) | copy-start | bytes 3076
  319.7 183.0 %copy-start.1 = (bf16[2048,2,128]{2,1,0:T(2,128)(2,1)S(1)}, bf16[2048,2,128]{2,1,0:T(2,128)(2,1)}, u32[]{:S(2)}) copy-start(bf16[2048,2,128]{2,1,0:T(2,128)(2,1)} %param.11) | copy-start | bytes 3145732
Sparse Core Ops, SparseCore 0:
  81.9 236.3 all-gather.1
where the time goes:
time: 512 us; the launch traced here: 509 us
  blocking collectives  153 us (30%)
  other arithmetic  134 us (26%)
  waiting for transfers between devices  129 us (25%)
  local copies, waits for them, and re-layouts  60.5 us (12%)
  matrix products  17.1 us (3%)
  between operations  13.5 us (3%)
    all_gather x1, waiting for transfers between devices, combined_all(): pieces = jax.tree.map(lambda part: lax.all_gather(part, axis), value)  129 us
    add x63, other arithmetic, combine_pair(): out_a * weight_a[..., None] + out_b * weight_b[..., None]  119 us
    all_gather x2, blocking collectives, combined_all(): pieces = jax.tree.map(lambda part: lax.all_gather(part, axis), value)  97.5 us
    all_gather x1, blocking collectives, per_device(): every_query = lax.all_gather(queries, 'seq', axis=0, tiled=True)  55 us
    slice x3, local copies, waits for them, and re-layouts, combined_all(): tail = jax.tree.map(lambda part: part[1:], pieces)  43.8 us
    dynamic_slice x189, local copies, waits for them, and re-layouts, combined_all(): lax.scan(lambda so_far, slab: (join(so_far, slab), None), head, tail)  13.2 us
  transfers between devices with their start and end apart: 1, of which 1 were waited for; matrix products, arithmetic and copies ran while one was open for 2% of the time, Pallas kernels for 0%

commit v1 on v0

v1 whole, which is shorter than its diff:
```python
import functools
import math

import jax
import jax.numpy as jnp
from jax import lax
from jax.experimental import pallas as pl
from jax.experimental.pallas import tpu as pltpu
from jax.sharding import PartitionSpec as P

MESH = pl.DeviceIdType.MESH
HD = 128
BLOCK = 512
NBLOCKS = 4
TOK = BLOCK * NBLOCKS
NEG = -1e30
SCALE2 = HD ** (-0.5) * math.log2(math.e)
F32 = jnp.float32
BF16 = jnp.bfloat16


def lanes_of(rows):
    return lax.broadcasted_iota(jnp.int32, (rows, 128), 1)


def encode(stat, count):
    stat = jnp.where(lanes_of(16) < count, stat, 0.0)
    high = stat.astype(BF16).astype(F32)
    rest = stat - high
    middle = rest.astype(BF16).astype(F32)
    low = rest - middle
    return high + pltpu.roll(middle, 32, 1) + pltpu.roll(low, 64, 1)


def decode(tile):
    tile = tile.astype(F32)
    return tile + pltpu.roll(tile, 96, 1) + pltpu.roll(tile, 64, 1)


def weights_of(stats):
    top = functools.reduce(jnp.maximum, stats)
    raw = [jnp.exp2(s - top) for s in stats]
    total = functools.reduce(jnp.add, raw)
    inverse = 1.0 / total
    return [w * inverse for w in raw], top + jnp.log2(total)


def two_columns(weight, g, column):
    part = weight[g * 8 : (g + 1) * 8]
    return jnp.concatenate(
        [jnp.broadcast_to(part[:, column + r : column + r + 1], (8, 128)) for r in range(2)], axis=0
    )


def kernel(
    ny, nz,
    q_ref, k_hbm, v_hbm, nk_ref, nv_ref, start_ref, count_ref, out_ref,
    qbuf, bias, kraw, vraw, temp, kaug, vaug, scores,
    core_out, core_in, y_out, y_in, z_out, z_in,
    load_sem, qz_send, qz_recv, qy_send, qy_recv, qc_send, qc_recv,
    c_send, c_recv, y_send, y_recv, z_send, z_recv,
):
    seq = lax.axis_index("seq")
    x = lax.axis_index("kvh")
    core = lax.rem(seq, 2)
    z = lax.rem(lax.div(seq, 2), nz)
    y = lax.div(seq, 2 * nz)
    other = 1 - core

    def device(yy, zz, cc):
        return ((yy * nz + zz) * 2 + cc, x)

    loads = [
        pltpu.make_async_copy(k_hbm, kraw, load_sem.at[0]),
        pltpu.make_async_copy(v_hbm, vraw, load_sem.at[1]),
    ]
    for load in loads:
        load.start()

    barrier = pltpu.get_barrier_semaphore()
    peers = (
        [device(y, lax.rem(z + k, nz), core) for k in range(1, nz)]
        + [device(lax.rem(y + k, ny), z, core) for k in range(1, ny)]
        + [device(y, z, other)]
    )
    for peer in peers:
        pl.semaphore_signal(barrier, inc=1, device_id=peer, device_id_type=MESH)

    q_own = q_ref[...].astype(F32)
    for g in range(2):
        qbuf[core, y, z, g] = jnp.concatenate(
            [q_own[r, g * 8 : (g + 1) * 8] for r in range(2)], axis=0
        ).astype(BF16)
    pl.semaphore_wait(barrier, len(peers))

    def remote(src, dst, send, recv, peer):
        return pltpu.make_async_remote_copy(
            src_ref=src, dst_ref=dst, send_sem=send, recv_sem=recv, device_id=peer, device_id_type=MESH
        )

    def qz_copy(k):
        mine = qbuf.at[core, y, z]
        return remote(mine, mine, qz_send.at[k - 1], qz_recv.at[k - 1], device(y, lax.rem(z + k, nz), core))

    def qz_arrival(k):
        there = qbuf.at[core, y, lax.rem(z - k + nz, nz)]
        return remote(there, there, qz_send.at[k - 1], qz_recv.at[k - 1], device(y, lax.rem(z + k, nz), core))

    for k in range(1, nz):
        qz_copy(k).start()

    block = seq * NBLOCKS + lanes_of(8)

    def row_bias(row):
        seen = None
        for i in range(2):
            first = start_ref[i, row]
            inside = (block >= first) & (block < first + count_ref[i, row])
            seen = inside if seen is None else seen | inside
        return jnp.where(seen | (lanes_of(8) >= NBLOCKS), 0.0, NEG)

    def fill_bias(source, carry):
        yy = lax.div(source, 2 * nz)
        zz = lax.rem(lax.div(source, 2), nz)
        cc = lax.rem(source, 2)
        bias[cc, yy, zz] = jnp.concatenate([row_bias(2 * source), row_bias(2 * source + 1)], axis=0).astype(BF16)
        return carry

    lax.fori_loop(0, 2 * ny * nz, fill_bias, 0)

    piece = 256
    for load in loads:
        load.wait()

    def split(i, carry):
        at = pl.multiple_of(i * piece, piece)
        flat = pl.multiple_of(i * 2 * piece, 2 * piece)
        indicator = (lanes_of(piece) == lax.div(at, BLOCK)).astype(F32).astype(BF16)
        temp[0] = kraw[pl.ds(flat, 2 * piece), :].astype(F32)
        temp[1] = vraw[pl.ds(flat, 2 * piece), :].astype(F32)
        for g in range(2):
            kaug[g, pl.ds(at, piece), 0:128] = temp[0, pl.ds(g, piece, stride=2), :].astype(BF16)
            kaug[g, pl.ds(at, piece), 128:256] = indicator
            vaug[g, pl.ds(at, piece), 0:128] = temp[1, pl.ds(g, piece, stride=2), :].astype(BF16)
            vaug[g, pl.ds(at, piece), 128:256] = jnp.ones((piece, 128), BF16)
        return carry

    lax.fori_loop(0, TOK // piece, split, 0)

    for k in range(1, nz):
        qz_arrival(k).wait_recv()

    def qy_copy(k):
        mine = qbuf.at[core, y]
        return remote(mine, mine, qy_send.at[k - 1], qy_recv.at[k - 1], device(lax.rem(y + k, ny), z, core))

    def qy_arrival(k):
        there = qbuf.at[core, lax.rem(y - k + ny, ny)]
        return remote(there, there, qy_send.at[k - 1], qy_recv.at[k - 1], device(lax.rem(y + k, ny), z, core))

    def qc_copy(i):
        mine = qbuf.at[core, lax.rem(y - i + ny, ny)]
        return remote(mine, mine, qc_send.at[i], qc_recv.at[i], device(y, z, other))

    def qc_arrival(i):
        there = qbuf.at[other, lax.rem(y - i + ny, ny)]
        return remote(there, there, qc_send.at[i], qc_recv.at[i], device(y, z, other))

    for k in range(1, ny):
        qy_copy(k).start()
    qc_copy(0).start()

    rows = 16 * nz

    def c_copy(i):
        yy = lax.rem(y - i + ny, ny)
        return remote(core_out.at[0, yy], core_in.at[yy], c_send.at[i], c_recv.at[i], device(y, z, other))

    def attend(yy):
        stats = [[None] * 2, [None] * 2]
        for g in range(2):
            lhs = jnp.concatenate(
                [
                    jnp.concatenate([qbuf[cc, yy, :, g].reshape(rows, 128), bias[cc, yy].reshape(rows, 128)], axis=1)
                    for cc in (other, core)
                ],
                axis=0,
            )
            top = None
            for b in range(NBLOCKS):
                s = lax.dot_general(
                    lhs, kaug[g, b * BLOCK : (b + 1) * BLOCK, :], (((1,), (1,)), ((), ())),
                    preferred_element_type=F32,
                )
                scores[g, :, b * BLOCK : (b + 1) * BLOCK] = s
                for i in range(BLOCK // 128):
                    part = s[:, i * 128 : (i + 1) * 128]
                    top = part if top is None else jnp.maximum(top, part)
            top = jnp.max(top, axis=1, keepdims=True)
            total = jnp.zeros((2 * rows, 256), F32)
            for b in range(NBLOCKS):
                s = scores[g, :, b * BLOCK : (b + 1) * BLOCK]
                p = jnp.exp2((s - top) * SCALE2).astype(BF16)
                total = total + jnp.dot(p, vaug[g, b * BLOCK : (b + 1) * BLOCK, :], preferred_element_type=F32)
            norm = total[:, 128:256]
            out = total[:, 0:128] * (1.0 / norm)
            stat = top * SCALE2 + jnp.log2(norm)
            for part in range(2):
                packed = jnp.zeros((8, 128), F32)
                for k in range(2 * nz):
                    at = part * rows + k * 8
                    packed = jnp.where(lanes_of(8) == k, stat[at : at + 8], packed)
                stats[part][g] = packed
                for zz in range(nz):
                    at = part * rows + zz * 16
                    core_out[part, yy, zz * 2 + g] = out[at : at + 16].astype(BF16)
        for part in range(2):
            core_out[part, yy, 2 * nz] = encode(jnp.concatenate(stats[part], axis=0), 2 * nz).astype(BF16)

    def merge(parts, put, put_stat):
        weights, stat = weights_of([decode(part[2 * nz]) for part in parts])
        for zz in range(nz):
            for g in range(2):
                tile = None
                for part, weight in zip(parts, weights):
                    term = part[zz * 2 + g].astype(F32) * two_columns(weight, g, 2 * zz)
                    tile = term if tile is None else tile + term
                put(zz, g, tile.astype(BF16))
        put_stat(encode(stat, 2 * nz))

    def y_copy(i):
        yy = lax.rem(y - i + ny, ny)
        return remote(y_out.at[yy], y_in.at[i - 1], y_send.at[i - 1], y_recv.at[i - 1], device(yy, z, core))

    def merge_cores(i):
        yy = lax.rem(y - i + ny, ny)
        c_copy(i).wait_recv()

        def put(zz, g, tile):
            y_out[yy, zz * 2 + g] = tile

        def put_stat(tile):
            y_out[yy, 2 * nz] = tile.astype(BF16)

        merge([core_out.at[1, yy], core_in.at[yy]], put, put_stat)

    def step(i, carry):
        @pl.when(i == 1)
        def _():
            for k in range(1, ny):
                qy_arrival(k).wait_recv()
                qc_copy(k).start()

        qc_arrival(i).wait_recv()
        attend(lax.rem(y - i + ny, ny))
        c_copy(i).start()

        @pl.when(i >= 1)
        def _():
            merge_cores(i - 1)

            @pl.when(i >= 2)
            def _():
                y_copy(i - 1).start()

        return carry

    lax.fori_loop(0, ny, step, 0)
    merge_cores(ny - 1)
    y_copy(ny - 1).start()

    for i in range(1, ny):
        y_copy(i).wait_recv()

    def put_z(zz, g, tile):
        z_out[zz, g] = tile

    def put_z_stat(tile):
        for zz in range(nz):
            z_out[zz, 2] = (tile if zz == 0 else pltpu.roll(tile, 128 - 2 * zz, 1)).astype(BF16)

    merge([y_out.at[y]] + [y_in.at[i] for i in range(ny - 1)], put_z, put_z_stat)

    def z_copy(k):
        zz = lax.rem(z + k, nz)
        return remote(z_out.at[zz], z_in.at[k - 1], z_send.at[k - 1], z_recv.at[k - 1], device(y, zz, core))

    for k in range(1, nz):
        z_copy(k).start()

    own = [None, None]
    for g in range(2):
        packed = jnp.zeros((8, 128), F32)
        for r in range(2):
            key = nk_ref[r].astype(F32)[g : g + 1]
            dots = jnp.sum(q_own[r, g * 8 : (g + 1) * 8] * key, axis=1, keepdims=True) * SCALE2
            packed = jnp.where(lanes_of(8) == r, dots, packed)
        own[g] = packed
    own = jnp.concatenate(own, axis=0)

    for k in range(1, nz):
        z_copy(k).wait_recv()

    parts = [z_out.at[z]] + [z_in.at[k] for k in range(nz - 1)]
    weights, _ = weights_of([decode(part[2]) for part in parts] + [own])
    tiles = []
    for g in range(2):
        tile = None
        for part, weight in zip(parts, weights):
            term = part[g].astype(F32) * two_columns(weight, g, 0)
            tile = term if tile is None else tile + term
        value = jnp.concatenate(
            [jnp.broadcast_to(nv_ref[r].astype(F32)[g : g + 1], (8, 128)) for r in range(2)], axis=0
        )
        tiles.append(tile + value * two_columns(weights[-1], g, 0))
    for r in range(2):
        out_ref[r] = jnp.concatenate([tiles[g][r * 8 : (r + 1) * 8] for g in range(2)], axis=0).astype(BF16)

    for k in range(1, nz):
        qz_copy(k).wait_send()
        z_copy(k).wait_send()
    for k in range(1, ny):
        qy_copy(k).wait_send()
        y_copy(k).wait_send()
    for i in range(ny):
        qc_copy(i).wait_send()
        c_copy(i).wait_send()


def per_device(ny, nz, queries, cache_keys, cache_values, new_keys, new_values, doc_start, doc_count):
    vmem = pl.BlockSpec(memory_space=pltpu.VMEM)
    smem = pl.BlockSpec(memory_space=pltpu.SMEM)
    hbm = pl.BlockSpec(memory_space=pl.ANY)
    dma = pltpu.SemaphoreType.DMA
    block = 2 * nz + 1
    return pl.pallas_call(
        functools.partial(kernel, ny, nz),
        out_shape=jax.ShapeDtypeStruct(queries.shape, BF16),
        in_specs=[vmem, hbm, hbm, vmem, vmem, smem, smem],
        out_specs=vmem,
        scratch_shapes=[
            pltpu.VMEM((2, ny, nz, 2, 16, 128), BF16),
            pltpu.VMEM((2, ny, nz, 16, 128), BF16),
            pltpu.VMEM((2 * TOK, 128), BF16),
            pltpu.VMEM((2 * TOK, 128), BF16),
            pltpu.VMEM((2, 512, 128), F32),
            pltpu.VMEM((2, TOK, 256), BF16),
            pltpu.VMEM((2, TOK, 256), BF16),
            pltpu.VMEM((2, 32 * nz, TOK), F32),
            pltpu.VMEM((2, ny, block, 16, 128), BF16),
            pltpu.VMEM((ny, block, 16, 128), BF16),
            pltpu.VMEM((ny, block, 16, 128), BF16),
            pltpu.VMEM((ny - 1, block, 16, 128), BF16),
            pltpu.VMEM((nz, 3, 16, 128), BF16),
            pltpu.VMEM((nz - 1, 3, 16, 128), BF16),
            dma((2,)),
            dma((nz - 1,)), dma((nz - 1,)),
            dma((ny - 1,)), dma((ny - 1,)),
            dma((ny,)), dma((ny,)),
            dma((ny,)), dma((ny,)),
            dma((ny - 1,)), dma((ny - 1,)),
            dma((nz - 1,)), dma((nz - 1,)),
        ],
        compiler_params=pltpu.CompilerParams(
            collective_id=0, has_side_effects=True, vmem_limit_bytes=60 * 1024 * 1024
        ),
        name="attention",
    )(
        queries,
        cache_keys.reshape(2 * TOK, 128),
        cache_values.reshape(2 * TOK, 128),
        new_keys,
        new_values,
        doc_start.T,
        doc_count.T,
    )


def solution(mesh):
    ny, nz = 4, mesh.shape["seq"] // 8
    placed = (P("seq", "kvh", None),) * 5 + (P(), P())
    return jax.shard_map(
        functools.partial(per_device, ny, nz),
        mesh=mesh,
        in_specs=placed,
        out_specs=P("seq", "kvh", None),
        check_vma=False,
    )
```

time: 512 us -> 41.1 us (0.08)
  blocking collectives: 153 us -> 0 us
  other arithmetic: 134 us -> 0 us
  waiting for transfers between devices: 129 us -> 0 us
  local copies, waits for them, and re-layouts: 60.5 us -> 1.3 us
  Pallas kernels: 0 us -> 39.6 us
  matrix products: 17.1 us -> 0 us
  between operations: 13.5 us -> 0.01 us
    all_gather x3 -> x0, blocking collectives: 153 us -> none  [the longest x2 97.5 us: combined_all(): pieces = jax.tree.map(lambda part: lax.all_gather(part, axis), value)]
    all_gather x1 -> x0, waiting for transfers between devices: 129 us -> none  [combined_all(): pieces = jax.tree.map(lambda part: lax.all_gather(part, axis), value)]
    add x129 -> x0, other arithmetic: 124 us -> none  [the longest x63 119 us: combine_pair(): out_a * weight_a[..., None] + out_b * weight_b[..., None]]
    slice x3 -> x0, local copies, waits for them, and re-layouts: 43.8 us -> none  [combined_all(): tail = jax.tree.map(lambda part: part[1:], pieces)]
    pallas_call x0 -> x1, Pallas kernels: none -> 39.6 us  [per_device(): pl.pallas_call(functools.partial(kernel, ny, nz), out_shape=jax.ShapeDtyp...]
    dot_general x3 -> x0, matrix products: 17.1 us -> none  [the longest x1 8.49 us: per_device(): jnp.einsum('gjrt,tgd->rgjd', probs.astype(jnp.bfloat16), cache_values, pr...]
    dynamic_slice x189 -> x0, local copies, waits for them, and re-layouts: 13.2 us -> none  [combined_all(): lax.scan(lambda so_far, slab: (join(so_far, slab), None), head, tail)]
    reduce_sum x1 -> x0, other arithmetic: 9.09 us -> none  [per_device(): total = jnp.sum(probs, axis=-1)]
  transfers between devices with their start and end apart: 1 -> 0, of which waited for: 1 -> 0; matrix products, arithmetic and copies ran while one was open for 2% -> 0% of each run, Pallas kernels for 0% -> 0%
where the time goes in v1:
time: 41.1 us; the launch traced here: 40.9 us
  Pallas kernels  39.6 us (96%)
  local copies, waits for them, and re-layouts  1.3 us (3%)
    pallas_call x1, Pallas kernels, per_device(): pl.pallas_call(functools.partial(kernel, ny, nz), out_shape=jax.ShapeDtyp...  39.6 us
    unnamed x1, local copies, waits for them, and re-layouts  1.3 us

profile of v1, /device:TPU:1, one launch (start us, length us, event | category | flops | bytes accessed | tf_op | source)
XLA Modules:
  0.0 40.9 jit_solution(16802812446655095307)
XLA Ops:
  0.0 39.6 %attention.1 = bf16[2,16,128]{2,1,0:T(8,128)(2,1)} custom-call(bf16[2,16,128]{2,1,0:T(8,128)(2,1)} %q_ref.1, bf16[4096,128]{1,0:T(8,128)(2,1)} %bitcast.4, bf16[4096,128]{1,0:T(8,128)(2,1)} %bitcast.5, bf16[2,2,128]{2,1,0:T(2,128)(2,1)} %nk_ref.1, bf16[2,2,128]{2,1,0:T(2,128)(2,1)} %nv_ref.1, s32[2,128]{1,0:T(2,128)} %bitcast.6, s32[2,128]{1,0:T(2,128)} %bitcast.7), custom_call_target="tpu_custom_call" | custom-call | tf_op jit(solution)/shard_map/attention/pallas_call | solution.py:336
  39.6 1.3 %copy.9 = bf16[2,16,128]{2,1,0:T(8,128)(2,1)} copy(bf16[2,16,128]{2,1,0:T(8,128)(2,1)} %attention.1) | data formatting | bytes 16384
